TPU v7x, 32 devices: a whole 2x2x4 slice. The times are simulated.
32 devices in a mesh: row: 8 (over z, x), col: 4 (over y, core).
Axes of the slice: x: 2, y: 2, z: 4, core: 2. Of those that a mesh axis runs over, the one named last changes fastest.
Arguments:
- features: float32 [4096, 128], P(('row', 'col')), may hold values from -6 to 6
- weight: float32 [128, 128], replicated, may hold values from -0.5 to 0.5
- degree: int32 [4096], P(('row', 'col')), may hold values from 1 to 64
- tiles: float32 [8, 4, 24, 128, 128], P('row', 'col'), may hold values from 0 to 6, as said below
- tile_coords: int32 [8, 4, 24, 2], P('row', 'col'), may hold values from 0 to 7, as said below
- tile_count: int32 [8, 4], P('row', 'col'), may hold values from 1 to 24, as said below
- cotangent: float32 [4096, 128], P(('row', 'col')), may hold values from -0.25 to 0.25
Outputs:
- hidden_out: float32 [4096, 128], P(('row', 'col'))
- weight_grad: float32 [128, 128], replicated
Inputs may be any that keep to these rules, and one draw needn't show every extreme that they name: `tiles`: only slots below tile_count are live; the other slots hold values that are ignored. `tile_coords`: the first entry is a tile row below 4, the second a tile column below 8; within one device the pairs of all slots are distinct. `tile_count`: number of live slots of a device; the largest is reached on some device.
All inputs are finite; a program needn't handle non-finite values.
Results may differ from a plain program's by a relative error of at most 0.0003.
Values sent between devices are 32-bit elements; how exact they have to be, the bound alone decides.
A program may use at most 64 MiB of HBM per device.

v0:
```python
import jax
import jax.numpy as jnp
from jax import lax
from jax.sharding import PartitionSpec as P


def local(features, weight, degree, tiles, tile_coords, tile_count, cotangent):
    exact_accumulate = lax.Precision.HIGHEST
    node_dev, feat_width = features.shape
    tile_set = tiles[0, 0]
    coords = tile_coords[0, 0]
    slot_count, tile_edge, unused_edge = tile_set.shape
    live_mask = (jnp.arange(slot_count, dtype=jnp.int32) < tile_count[0, 0]).astype(jnp.float32)[
        :, None, None
    ]
    row_tiles = lax.axis_size("col") * node_dev // tile_edge
    col_tiles = lax.axis_size("row") * node_dev // tile_edge
    row_onehot = (coords[:, 0][None, :] == jnp.arange(row_tiles, dtype=jnp.int32)[:, None]).astype(
        jnp.float32
    )
    inv_root = lax.rsqrt(degree.astype(jnp.float32))[:, None]
    outgoing = features * inv_root
    col_block = lax.all_gather(outgoing, "row", axis=0, tiled=True).reshape(
        col_tiles, tile_edge, feat_width
    )
    picked = col_block[coords[:, 1]]
    tile_products = (
        jnp.einsum("tab,tbf->taf", tile_set, picked, precision=exact_accumulate) * live_mask
    )
    row_partial = jnp.einsum("rt,taf->raf", row_onehot, tile_products, precision=exact_accumulate)
    row_partial = row_partial.reshape(row_tiles * tile_edge, feat_width)
    own_rows = lax.psum_scatter(row_partial, "col", scatter_dimension=0, tiled=True) * inv_root
    aggregated = jnp.dot(
        own_rows, weight, precision=exact_accumulate, preferred_element_type=jnp.float32
    )
    hidden_out = jax.nn.elu(aggregated)
    slope_grad = cotangent * jnp.exp(jnp.minimum(aggregated, 0.0))
    local_grad = jnp.dot(
        own_rows.T, slope_grad, precision=exact_accumulate, preferred_element_type=jnp.float32
    )
    weight_grad = lax.psum(local_grad, ("row", "col"))
    return (hidden_out, weight_grad)


def solution(mesh):
    return jax.shard_map(
        local,
        mesh=mesh,
        in_specs=(
            P(("row", "col"), None),
            P(),
            P(("row", "col")),
            P("row", "col", None, None, None),
            P("row", "col", None, None),
            P("row", "col"),
            P(("row", "col"), None),
        ),
        out_specs=(P(("row", "col"), None), P()),
        check_vma=False,
    )
```

profile of v0, /device:TPU:0, one launch (start us, length us, event | category | flops | bytes accessed | tf_op | source)
XLA Modules:
  0.0 208.3 jit_solution(10059342607016602286)
XLA Ops:
  7.2 0.0 copy-start
  7.2 0.0 reduce-scatter.2.cloned.1.call-start
  7.2 0.8 convert_rsqrt_fusion
  8.0 0.9 broadcast_multiply_fusion
  8.9 33.0 %all_gather.3 = f32[1024,128]{1,0:T(8,128)S(1)} all-gather(f32[128,128]{1,0:T(8,128)S(1)} %broadcast_multiply_fusion), channel_id=1, replica_groups=mesh['row'=8,'col'=4] {'row'}, dimensions={0}, use_global_device_ids=true | all-gather | bytes 589824 | tf_op jit(solution)/shard_map/all_gather | solution.py:23
  41.9 0.8 slice_bitcast_fusion
  42.7 1.8 gather_fusion
  44.5 0.0 copy-done
  44.5 5.2 %fusion.2 = f32[24,128,128]{2,1,0:T(8,128)} fusion(f32[24,128,128]{2,1,0:T(8,128)} %gather_fusion, f32[1,1,24,128,128]{4,3,2,1,0:T(8,128)S(1)} %copy-done), kind=kOutput, calls=%fused_computation.3 | convolution fusion | flops 603979776 | bytes 4718592 | tf_op jit(solution)/shard_map/tab,tbf->taf/dot_general | solution.py:28
  49.7 2.0 copy.10
  51.7 0.0 copy-start.1
  51.7 0.0 copy-start.2
  52.4 0.8 fusion
  53.2 0.7 copy.9
  53.9 0.0 reduce-scatter.2.cloned.1.call-update
  54.0 0.0 all-reduce.2.cloned.1.call-start
  54.0 21.2 %reduce-scatter.2.cloned.1.call-done = f32[128,128]{1,0:T(8,128)} async-done(((f32[512,128]{1,0:T(8,128)}), f32[128,128]{1,0:T(8,128)}) %reduce-scatter.2.cloned.1.call-update) | async-done | bytes 65552 | tf_op jit(solution)/shard_map/reduce_scatter | solution.py:32
  75.2 0.0 copy-done.1
  75.2 1.7 compare_select_fusion
  77.0 0.0 copy-done.2
  77.0 1.8 fusion.7
  78.8 0.0 all-reduce.2.cloned.1.call-update
  78.8 121.1 %all-reduce.2.cloned.1.call-done = f32[128,128]{1,0:T(8,128)} async-done(((f32[128,128]{1,0:T(8,128)}), f32[128,128]{1,0:T(8,128)}) %all-reduce.2.cloned.1.call-update) | async-done | bytes 65552 | tf_op jit(solution)/shard_map/psum | solution.py:41
  200.0 1.5 copy.13
  (2 shorter events, 0.0 us)
Async XLA Ops:
  7.2 37.4 %copy-start = (f32[1,1,24,128,128]{4,3,2,1,0:T(8,128)S(1)}, f32[1,1,24,128,128]{4,3,2,1,0:T(8,128)}, u32[]{:S(2)}) copy-start(f32[1,1,24,128,128]{4,3,2,1,0:T(8,128)} %param.10) | copy-start | bytes 4718596
  7.2 68.1 %reduce-scatter.2.cloned.1.call-start = ((), (), s32[]{:S(2)}) async-start(), calls=%async_computation.1 | async-start | bytes 327680 | tf_op jit(solution)/shard_map/reduce_scatter | solution.py:32
  51.7 23.6 %copy-start.1 = (f32[128,128]{1,0:T(8,128)S(1)}, f32[128,128]{1,0:T(8,128)}, u32[]{:S(2)}) copy-start(f32[128,128]{1,0:T(8,128)} %param.8) | copy-start | bytes 196612
  51.7 25.3 %copy-start.2 = (f32[128,128]{1,0:T(8,128)S(1)}, f32[128,128]{1,0:T(8,128)}, u32[]{:S(2)}) copy-start(f32[128,128]{1,0:T(8,128)} %param.13) | copy-start | bytes 196612
  54.0 146.0 %all-reduce.2.cloned.1.call-start = ((), (), s32[]{:S(2)}) async-start(), calls=%async_computation.2 | async-start | bytes 131072 | tf_op jit(solution)/shard_map/psum | solution.py:41
Sparse Core Ops, SparseCore 0:
  54.1 21.1 reduce-scatter.1
  82.3 117.5 all-reduce.1
where the time goes:
time: 210 us; the launch traced here: 208 us
  waiting for transfers between devices  142 us (68%)
  blocking collectives  33 us (16%)
  between operations  14.8 us (7%)
  matrix products  9.59 us (5%)
  local copies, waits for them, and re-layouts  5.97 us (3%)
  other arithmetic  2.46 us (1%)
    psum x1, waiting for transfers between devices, local(): weight_grad = lax.psum(local_grad, ('row', 'col'))  121 us
    all_gather x1, blocking collectives, local(): lax.all_gather(outgoing, 'row', axis=0, tiled=True)  33 us
    reduce_scatter x1, waiting for transfers between devices, local(): lax.psum_scatter(row_partial, 'col', scatter_dimension=0, tiled=True)  21.2 us
    dot_general x1, matrix products, local(): jnp.einsum('tab,tbf->taf', tile_set, picked, precision=exact_accumulate)  5.21 us
  transfers between devices with their start and end apart: 2, of which 2 were waited for; matrix products, arithmetic and copies ran while one was open for 0% of the time, Pallas kernels for 0%

commit v1 on v0

--- a/solution.py
+++ b/solution.py
@@ -1,10 +1,18 @@
+import functools
+
 import jax
 import jax.numpy as jnp
 from jax import lax
+from jax.experimental import pallas as pl
+from jax.experimental.pallas import tpu as pltpu
 from jax.sharding import PartitionSpec as P
 
-
-def local(features, weight, degree, tiles, tile_coords, tile_count, cotangent):
+F32 = jnp.float32
+BF16 = jnp.bfloat16
+MESH = pl.DeviceIdType.MESH
+
+
+def gathered(features, weight, degree, tiles, tile_coords, tile_count, cotangent):
     exact_accumulate = lax.Precision.HIGHEST
     node_dev, feat_width = features.shape
     tile_set = tiles[0, 0]
@@ -42,7 +50,344 @@
     return (hidden_out, weight_grad)
 
 
+def halves(v):
+    hi = v.astype(BF16)
+    return hi, (v - hi.astype(F32)).astype(BF16)
+
+
+def dot(a, b, dims=((1,), (0,))):
+    return lax.dot_general(a, b, (dims, ((), ())), preferred_element_type=F32)
+
+
+def dot_split(a, b, dims=((1,), (0,))):
+    a_hi, a_lo = halves(a)
+    b_hi, b_lo = halves(b)
+    return dot(a_hi, b_hi, dims) + dot(a_hi, b_lo, dims) + dot(a_lo, b_hi, dims)
+
+
+def fused(
+    n_row,
+    features,
+    weight,
+    degree,
+    tiles_hbm,
+    coords,
+    count,
+    cotangent,
+    hidden_out,
+    weight_grad,
+    tiles,
+    nodes,
+    a_hi,
+    a_lo,
+    acc,
+    from_core,
+    to_y,
+    from_y,
+    grad,
+    terms,
+    total,
+    grad_all,
+    codes,
+    tile_sem,
+    up_sem,
+    down_sem,
+    across_sem,
+    node_sem,
+    core_send,
+    core_recv,
+    y_send,
+    y_recv,
+    term_send,
+    term_recv,
+    all_send,
+    all_recv,
+):
+    n_col = 4
+    nz = n_row // 2
+    n_dev = n_row * n_col
+    slots = tiles.shape[0]
+    width = features.shape[0]
+    i = lax.axis_index("row")
+    j = lax.axis_index("col")
+    me = i * n_col + j
+    z = i // 2
+    x = i % 2
+    y = j // 2
+    core = j % 2
+
+    def device(d):
+        return {"row": d // n_col, "col": d % n_col}
+
+    load_tiles = pltpu.make_async_copy(tiles_hbm.at[0, 0], tiles, tile_sem)
+    load_tiles.start()
+
+    barrier = pltpu.get_barrier_semaphore()
+
+    @pl.loop(1, n_dev)
+    def _(k):
+        pl.semaphore_signal(
+            barrier, inc=1, device_id=device((me + k) % n_dev), device_id_type=MESH
+        )
+
+    inv_row = lax.rsqrt(degree[...].astype(F32))
+    eye = lax.broadcasted_iota(jnp.int32, (width, width), 0) == lax.broadcasted_iota(
+        jnp.int32, (width, width), 1
+    )
+    inv_root = jnp.sum(
+        jnp.where(eye, jnp.broadcast_to(inv_row, (width, width)), 0.0), axis=1, keepdims=True
+    )
+    nodes[z, pl.ds(pl.multiple_of(x * width, width), width)] = features[...] * inv_root
+    pl.semaphore_wait(barrier, n_dev - 1)
+
+    def block(zz, xx):
+        return nodes.at[zz, pl.ds(pl.multiple_of(xx * width, width), width)]
+
+    def send(zz, to_row, sem):
+        return pltpu.make_async_remote_copy(
+            src_ref=block(zz, x),
+            dst_ref=block(zz, x),
+            send_sem=sem,
+            recv_sem=node_sem.at[zz, x],
+            device_id={"row": to_row, "col": j},
+            device_id_type=MESH,
+        )
+
+    def arrive(zz, xx):
+        pltpu.make_async_copy(block(zz, xx), block(zz, xx), node_sem.at[zz, xx]).wait()
+
+    def pass_on(zz, s, upward, downward):
+        send(zz, i - x + (1 - x), across_sem.at[zz]).start()
+        if upward:
+
+            @pl.when(z + 1 < nz)
+            def _():
+                send(zz, i + 2, up_sem.at[s]).start()
+
+        if downward:
+
+            @pl.when(z > 0)
+            def _():
+                send(zz, i - 2, down_sem.at[s]).start()
+
+    pass_on(z, 0, True, True)
+
+    for t in range(slots):
+        live = t < count[0, 0]
+        codes[t] = jnp.where(live, coords[0, 0, t, 0] * n_row + coords[0, 0, t, 1], -1)
+    load_tiles.wait()
+
+    @pl.loop(0, nz)
+    def _(zz):
+        for xx in range(2):
+            for r in range(n_col):
+                code = r * n_row + zz * 2 + xx
+                slot = jnp.int32(-1)
+                for t in range(slots):
+                    slot = jnp.where(codes[t] == code, jnp.int32(t), slot)
+                tile = tiles[jnp.maximum(slot, 0)]
+                hi, lo = halves(jnp.where(slot >= 0, tile, 0.0))
+                a_hi[zz, r * width : (r + 1) * width, xx * width : (xx + 1) * width] = hi
+                a_lo[zz, r * width : (r + 1) * width, xx * width : (xx + 1) * width] = lo
+
+    acc[...] = jnp.zeros_like(acc)
+
+    def multiply(zz):
+        x_hi, x_lo = halves(nodes[zz])
+        acc[...] += dot(a_hi[zz], x_hi) + dot(a_hi[zz], x_lo) + dot(a_lo[zz], x_hi)
+
+    for s in range(nz):
+        if s > 0:
+
+            @pl.when(z - s >= 0)
+            def _():
+                arrive(z - s, x)
+                pass_on(z - s, s, True, False)
+
+            @pl.when(z + s < nz)
+            def _():
+                arrive(z + s, x)
+                pass_on(z + s, s, False, True)
+
+        if s == 0:
+            arrive(z, 1 - x)
+            multiply(z)
+        else:
+
+            @pl.when(z - s >= 0)
+            def _():
+                arrive(z - s, 1 - x)
+                multiply(z - s)
+
+            @pl.when(z + s < nz)
+            def _():
+                arrive(z + s, 1 - x)
+                multiply(z + s)
+
+    def part(k):
+        return acc.at[pl.ds(pl.multiple_of(k * width, width), width)]
+
+    def to_core(yy):
+        return pltpu.make_async_remote_copy(
+            src_ref=part(yy * 2 + 1 - core),
+            dst_ref=from_core.at[yy],
+            send_sem=core_send.at[yy],
+            recv_sem=core_recv.at[yy],
+            device_id={"row": i, "col": y * 2 + 1 - core},
+            device_id_type=MESH,
+        )
+
+    far_core = to_core(1 - y)
+    own_core = to_core(y)
+    far_core.start()
+    own_core.start()
+    far_core.wait_recv()
+    to_y[...] = part((1 - y) * 2 + core)[...] + from_core[1 - y]
+    y_copy = pltpu.make_async_remote_copy(
+        src_ref=to_y,
+        dst_ref=from_y,
+        send_sem=y_send,
+        recv_sem=y_recv,
+        device_id={"row": i, "col": (1 - y) * 2 + core},
+        device_id_type=MESH,
+    )
+    y_copy.start()
+    own_core.wait_recv()
+    own_sum = part(j)[...] + from_core[y]
+    y_copy.wait_recv()
+    own_rows = (own_sum + from_y[...]) * inv_root
+    aggregated = dot_split(own_rows, weight[...])
+    grown = jnp.exp(jnp.minimum(aggregated, 0.0))
+    slope = cotangent[...] * grown
+    local_grad = dot_split(own_rows, slope, ((0,), (0,)))
+    rows = width // n_dev
+    grad[...] = local_grad.reshape(n_dev, rows, width)
+
+    @pl.loop(1, n_dev)
+    def _(k):
+        d = (me + k) % n_dev
+        pltpu.make_async_remote_copy(
+            src_ref=grad.at[d],
+            dst_ref=terms.at[n_dev - 1 - k],
+            send_sem=term_send,
+            recv_sem=term_recv,
+            device_id=device(d),
+            device_id_type=MESH,
+        ).start()
+
+    hidden_out[...] = jnp.where(aggregated > 0.0, aggregated, grown - 1.0)
+    pltpu.make_async_copy(terms, terms, term_recv).wait()
+    total[...] = grad[me] + jnp.sum(terms[...], axis=0)
+
+    @pl.loop(1, n_dev)
+    def _(k):
+        d = (me + k) % n_dev
+        pltpu.make_async_remote_copy(
+            src_ref=total,
+            dst_ref=grad_all.at[me],
+            send_sem=all_send,
+            recv_sem=all_recv,
+            device_id=device(d),
+            device_id_type=MESH,
+        ).start()
+
+    pltpu.make_async_copy(terms, terms, all_recv).wait()
+    grad_all[me] = total[...]
+    weight_grad[...] = grad_all[...].reshape(width, width)
+
+    pltpu.make_async_copy(terms, terms, term_send).wait()
+    pltpu.make_async_copy(terms, terms, all_send).wait()
+    send(z, i, across_sem.at[z]).wait_send()
+    far_core.wait_send()
+    own_core.wait_send()
+    y_copy.wait_send()
+
+    def sent(sem):
+        pltpu.make_async_copy(block(0, 0), block(0, 0), sem).wait()
+
+    for s in range(nz):
+        if s > 0:
+
+            @pl.when(z - s >= 0)
+            def _():
+                sent(across_sem.at[z - s])
+
+            @pl.when(z + s < nz)
+            def _():
+                sent(across_sem.at[z + s])
+
+        @pl.when((z - s >= 0) & (z + 1 < nz))
+        def _():
+            sent(up_sem.at[s])
+
+        @pl.when((z + s < nz) & (z > 0))
+        def _():
+            sent(down_sem.at[s])
+
+
+def dense(features, weight, degree, tiles, tile_coords, tile_count, cotangent):
+    n_row = lax.axis_size("row")
+    n_col = lax.axis_size("col")
+    n_dev = n_row * n_col
+    nz = n_row // 2
+    width, feat = features.shape
+    slots = tiles.shape[2]
+    rows = width // n_dev
+    vmem = pl.BlockSpec(memory_space=pltpu.VMEM)
+    smem = pl.BlockSpec(memory_space=pltpu.SMEM)
+    dma = pltpu.SemaphoreType.DMA
+    return pl.pallas_call(
+        functools.partial(fused, n_row),
+        out_shape=(
+            jax.ShapeDtypeStruct((width, feat), F32),
+            jax.ShapeDtypeStruct((feat, feat), F32),
+        ),
+        in_specs=[vmem, vmem, vmem, pl.BlockSpec(memory_space=pl.ANY), smem, smem, vmem],
+        out_specs=(vmem, vmem),
+        scratch_shapes=[
+            pltpu.VMEM((slots, width, width), F32),
+            pltpu.VMEM((nz, 2 * width, feat), F32),
+            pltpu.VMEM((nz, n_col * width, 2 * width), BF16),
+            pltpu.VMEM((nz, n_col * width, 2 * width), BF16),
+            pltpu.VMEM((n_col * width, feat), F32),
+            pltpu.VMEM((2, width, feat), F32),
+            pltpu.VMEM((width, feat), F32),
+            pltpu.VMEM((width, feat), F32),
+            pltpu.VMEM((n_dev, rows, feat), F32),
+            pltpu.VMEM((n_dev - 1, rows, feat), F32),
+            pltpu.VMEM((rows, feat), F32),
+            pltpu.VMEM((n_dev, rows, feat), F32),
+            pltpu.SMEM((slots,), jnp.int32),
+            dma,
+            dma((nz,)),
+            dma((nz,)),
+            dma((nz,)),
+            dma((nz, 2)),
+            dma((2,)),
+            dma((2,)),
+            dma,
+            dma,
+            dma,
+            dma,
+            dma,
+            dma,
+        ],
+        compiler_params=pltpu.CompilerParams(
+            collective_id=0, has_side_effects=True, vmem_limit_bytes=32 * 1024 * 1024
+        ),
+    )(features, weight, degree.reshape(1, width), tiles, tile_coords, tile_count, cotangent)
+
+
 def solution(mesh):
+    n_row, n_col = mesh.shape["row"], mesh.shape["col"]
+
+    def local(features, weight, degree, tiles, tile_coords, tile_count, cotangent):
+        width, feat = features.shape
+        small = n_row * n_col <= 2 * tiles.shape[2] and n_row % 2 == 0 and n_col == 4
+        small = small and tiles.shape[3] == width and width % (n_row * n_col) == 0
+        form = dense if small and feat == width else gathered
+        return form(features, weight, degree, tiles, tile_coords, tile_count, cotangent)
+
     return jax.shard_map(
         local,
         mesh=mesh,

time: 210 us -> 44.8 us (0.21)
  waiting for transfers between devices: 142 us -> 0 us
  Pallas kernels: 0 us -> 36.6 us
  blocking collectives: 33 us -> 0 us
  between operations: 14.8 us -> 1.29 us
  matrix products: 9.59 us -> 0 us
  other arithmetic: 2.46 us -> 0 us
    psum x1 -> x0, waiting for transfers between devices: 121 us -> none  [local(): weight_grad = lax.psum(local_grad, ('row', 'col'))]
    pallas_call x0 -> x1, Pallas kernels: none -> 36.6 us  [dense(): pl.pallas_call(functools.partial(fused, n_row), out_shape=(jax.ShapeDtype...]
    all_gather x1 -> x0, blocking collectives: 33 us -> none  [local(): lax.all_gather(outgoing, 'row', axis=0, tiled=True)]
    reduce_scatter x1 -> x0, waiting for transfers between devices: 21.2 us -> none  [local(): lax.psum_scatter(row_partial, 'col', scatter_dimension=0, tiled=True)]
    dot_general x4 -> x0, matrix products: 9.59 us -> none  [the longest x1 5.21 us: local(): jnp.einsum('tab,tbf->taf', tile_set, picked, precision=exact_accumulate)]
    unnamed x7 -> x13, local copies, waits for them, and re-layouts: 1.49 us -> 6.6 us
    dot_general x2 -> x0, local copies, waits for them, and re-layouts: 2.67 us -> none  [the longest x1 1.95 us: local(): jnp.einsum('tab,tbf->taf', tile_set, picked, precision=exact_accumulate)]
  transfers between devices with their start and end apart: 2 -> 0, of which waited for: 2 -> 0; matrix products, arithmetic and copies ran while one was open for 0% -> 0% of each run, Pallas kernels for 0% -> 0%
where the time goes in v1:
time: 44.8 us; the launch traced here: 44.4 us
  Pallas kernels  36.6 us (82%)
  local copies, waits for them, and re-layouts  6.6 us (15%)
  between operations  1.29 us (3%)
    pallas_call x1, Pallas kernels, dense(): pl.pallas_call(functools.partial(fused, n_row), out_shape=(jax.ShapeDtype...  36.6 us
    unnamed x13, local copies, waits for them, and re-layouts  6.6 us

profile of v1, /device:TPU:0, one launch (start us, length us, event | category | flops | bytes accessed | tf_op | source)
XLA Modules:
  0.0 44.4 jit_solution(10249215140838314884)
XLA Ops:
  1.3 0.8 %copy.9.coords = s32[1,1,24,2]{3,2,1,0:T(8,128)S(1)} copy(s32[1,1,24,2]{2,3,1,0:T(2,128)} %param.11) | data formatting | bytes 384 | tf_op args[4]
  2.0 0.0 copy-start
  2.0 1.4 %copy-done = f32[1,1,24,128,128]{4,3,2,1,0:T(8,128)S(1)} copy-done((f32[1,1,24,128,128]{4,3,2,1,0:T(8,128)S(1)}, f32[1,1,24,128,128]{4,3,2,1,0:T(8,128)}, u32[]{:S(2)}) %copy-start) | copy-done | bytes 1572888
  3.4 0.0 copy-start.1
  3.4 0.8 %copy-done.1 = f32[128,128]{1,0:T(8,128)S(1)} copy-done((f32[128,128]{1,0:T(8,128)S(1)}, f32[128,128]{1,0:T(8,128)}, u32[]{:S(2)}) %copy-start.1) | copy-done | bytes 65560
  4.3 0.0 copy-start.2
  4.3 0.8 %copy-done.2 = f32[128,128]{1,0:T(8,128)S(1)} copy-done((f32[128,128]{1,0:T(8,128)S(1)}, f32[128,128]{1,0:T(8,128)}, u32[]{:S(2)}) %copy-start.2) | copy-done | bytes 65560
  5.1 0.0 copy-start.3
  5.1 0.8 %copy-done.3 = f32[128,128]{1,0:T(8,128)S(1)} copy-done((f32[128,128]{1,0:T(8,128)S(1)}, f32[128,128]{1,0:T(8,128)}, u32[]{:S(2)}) %copy-start.3) | copy-done | bytes 65560
  6.0 0.0 copy-start.4
  6.0 0.7 %copy-done.4 = s32[128]{0:T(128)S(1)} copy-done((s32[128]{0:T(128)S(1)}, s32[128]{0:T(128)}, u32[]{:S(2)}) %copy-start.4) | copy-done | bytes 536
  6.6 36.6 %shard_map.86 = (f32[128,128]{1,0:T(8,128)S(1)}, f32[128,128]{1,0:T(8,128)S(1)}) custom-call(f32[128,128]{1,0:T(8,128)S(1)} %copy-done.1, f32[128,128]{1,0:T(8,128)S(1)} %copy-done.2, s32[1,128]{1,0:T(1,128)S(1)} %bitcast.1, f32[1,1,24,128,128]{4,3,2,1,0:T(8,128)S(1)} %copy-done, s32[1,1,24,2]{3,2,1,0:T(8,128)S(1)} %copy.9.coords, s32[1,1]{1,0:T(1,128)S(6)} %copy.12.count, ...), custom_call_target="tpu_custom_call" | custom-call | tf_op jit(solution)/shard_map/pallas_call | solution.py:339
  43.2 0.6 %copy.13 = f32[128,128]{1,0:T(8,128)} copy(f32[128,128]{1,0:T(8,128)S(1)} %get-tuple-element.4) | data formatting | bytes 131072
  43.8 0.6 %copy.14 = f32[128,128]{1,0:T(8,128)} copy(f32[128,128]{1,0:T(8,128)S(1)} %get-tuple-element.5) | data formatting | bytes 131072
Async XLA Ops:
  2.0 1.4 %copy-start = (f32[1,1,24,128,128]{4,3,2,1,0:T(8,128)S(1)}, f32[1,1,24,128,128]{4,3,2,1,0:T(8,128)}, u32[]{:S(2)}) copy-start(f32[1,1,24,128,128]{4,3,2,1,0:T(8,128)} %tiles_hbm.1) | copy-start | bytes 4718596
  3.4 0.8 %copy-start.1 = (f32[128,128]{1,0:T(8,128)S(1)}, f32[128,128]{1,0:T(8,128)}, u32[]{:S(2)}) copy-start(f32[128,128]{1,0:T(8,128)} %features.1) | copy-start | bytes 196612
  4.3 0.8 %copy-start.2 = (f32[128,128]{1,0:T(8,128)S(1)}, f32[128,128]{1,0:T(8,128)}, u32[]{:S(2)}) copy-start(f32[128,128]{1,0:T(8,128)} %weight.1) | copy-start | bytes 196612
  5.1 0.8 %copy-start.3 = (f32[128,128]{1,0:T(8,128)S(1)}, f32[128,128]{1,0:T(8,128)}, u32[]{:S(2)}) copy-start(f32[128,128]{1,0:T(8,128)} %cotangent.1) | copy-start | bytes 196612
  6.0 0.7 %copy-start.4 = (s32[128]{0:T(128)S(1)}, s32[128]{0:T(128)}, u32[]{:S(2)}) copy-start(s32[128]{0:T(128)} %param.9) | copy-start | bytes 1540

commit v2 on v1

--- a/solution.py
+++ b/solution.py
@@ -67,15 +67,19 @@
 
 def fused(
     n_row,
+    features_hbm,
+    weight_hbm,
+    degree_hbm,
+    tiles_hbm,
+    coords,
+    count,
+    cotangent_hbm,
+    hidden_out,
+    weight_grad,
     features,
     weight,
     degree,
-    tiles_hbm,
-    coords,
-    count,
     cotangent,
-    hidden_out,
-    weight_grad,
     tiles,
     nodes,
     a_hi,
@@ -86,12 +90,10 @@
     from_y,
     grad,
     terms,
-    total,
-    grad_all,
+    layers,
     codes,
-    tile_sem,
-    up_sem,
-    down_sem,
+    load_sem,
+    line_sem,
     across_sem,
     node_sem,
     core_send,
@@ -100,12 +102,13 @@
     y_recv,
     term_send,
     term_recv,
+    layer_send,
+    layer_recv,
     all_send,
     all_recv,
 ):
     n_col = 4
     nz = n_row // 2
-    n_dev = n_row * n_col
     slots = tiles.shape[0]
     width = features.shape[0]
     i = lax.axis_index("row")
@@ -116,20 +119,31 @@
     y = j // 2
     core = j % 2
 
-    def device(d):
-        return {"row": d // n_col, "col": d % n_col}
-
-    load_tiles = pltpu.make_async_copy(tiles_hbm.at[0, 0], tiles, tile_sem)
-    load_tiles.start()
+    loads = [
+        pltpu.make_async_copy(source, target, load_sem.at[k])
+        for k, (source, target) in enumerate(
+            (
+                (degree_hbm, degree),
+                (features_hbm, features),
+                (tiles_hbm.at[0, 0], tiles),
+                (weight_hbm, weight),
+                (cotangent_hbm, cotangent),
+            )
+        )
+    ]
+    for load in loads:
+        load.start()
 
     barrier = pltpu.get_barrier_semaphore()
 
-    @pl.loop(1, n_dev)
-    def _(k):
-        pl.semaphore_signal(
-            barrier, inc=1, device_id=device((me + k) % n_dev), device_id_type=MESH
-        )
-
+    friends = [{"row": (i + 2 * s) % n_row, "col": j} for s in range(1, nz)]
+    friends.append({"row": z * 2 + 1 - x, "col": j})
+    friends.append({"row": i, "col": y * 2 + 1 - core})
+    friends.append({"row": i, "col": (1 - y) * 2 + core})
+    for friend in friends:
+        pl.semaphore_signal(barrier, inc=1, device_id=friend, device_id_type=MESH)
+
+    loads[0].wait()
     inv_row = lax.rsqrt(degree[...].astype(F32))
     eye = lax.broadcasted_iota(jnp.int32, (width, width), 0) == lax.broadcasted_iota(
         jnp.int32, (width, width), 1
@@ -137,45 +151,52 @@
     inv_root = jnp.sum(
         jnp.where(eye, jnp.broadcast_to(inv_row, (width, width)), 0.0), axis=1, keepdims=True
     )
+    loads[1].wait()
     nodes[z, pl.ds(pl.multiple_of(x * width, width), width)] = features[...] * inv_root
-    pl.semaphore_wait(barrier, n_dev - 1)
-
-    def block(zz, xx):
-        return nodes.at[zz, pl.ds(pl.multiple_of(xx * width, width), width)]
-
-    def send(zz, to_row, sem):
+    pl.semaphore_wait(barrier, len(friends))
+
+    step = width // 2
+
+    def block(zz, xx, h):
+        return nodes.at[zz, pl.ds(pl.multiple_of(xx * width + h * step, step), step)]
+
+    def send(zz, h, to_row, sem):
         return pltpu.make_async_remote_copy(
-            src_ref=block(zz, x),
-            dst_ref=block(zz, x),
+            src_ref=block(zz, x, h),
+            dst_ref=block(zz, x, h),
             send_sem=sem,
-            recv_sem=node_sem.at[zz, x],
+            recv_sem=node_sem.at[zz, x, h],
             device_id={"row": to_row, "col": j},
             device_id_type=MESH,
         )
 
-    def arrive(zz, xx):
-        pltpu.make_async_copy(block(zz, xx), block(zz, xx), node_sem.at[zz, xx]).wait()
-
-    def pass_on(zz, s, upward, downward):
-        send(zz, i - x + (1 - x), across_sem.at[zz]).start()
-        if upward:
-
-            @pl.when(z + 1 < nz)
-            def _():
-                send(zz, i + 2, up_sem.at[s]).start()
-
-        if downward:
-
-            @pl.when(z > 0)
-            def _():
-                send(zz, i - 2, down_sem.at[s]).start()
-
-    pass_on(z, 0, True, True)
+    def arrive(zz, xx, h):
+        pltpu.make_async_copy(block(zz, xx, h), block(zz, xx, h), node_sem.at[zz, xx, h]).wait()
+
+    def at_distance(s, act):
+        @pl.when(z + s < nz)
+        def _():
+            act(z + s)
+
+        @pl.when(z - s >= 0)
+        def _():
+            act(z - s)
+
+    def across(zz, h):
+        send(zz, h, z * 2 + 1 - x, across_sem.at[zz, h]).start()
+
+    for h in range(2):
+        across(z, h)
+    for s in range(nz - 1, 0, -1):
+        for h in range(2):
+            at_distance(s, lambda t, h=h: send(z, h, t * 2 + x, line_sem.at[t, h]).start())
 
     for t in range(slots):
         live = t < count[0, 0]
-        codes[t] = jnp.where(live, coords[0, 0, t, 0] * n_row + coords[0, 0, t, 1], -1)
-    load_tiles.wait()
+        codes[t] = jnp.where(live, coords[0, t] * n_row + coords[1, t], -1)
+    loads[2].wait()
+    loads[3].wait()
+    loads[4].wait()
 
     @pl.loop(0, nz)
     def _(zz):
@@ -196,33 +217,21 @@
         x_hi, x_lo = halves(nodes[zz])
         acc[...] += dot(a_hi[zz], x_hi) + dot(a_hi[zz], x_lo) + dot(a_lo[zz], x_hi)
 
-    for s in range(nz):
-        if s > 0:
-
-            @pl.when(z - s >= 0)
-            def _():
-                arrive(z - s, x)
-                pass_on(z - s, s, True, False)
-
-            @pl.when(z + s < nz)
-            def _():
-                arrive(z + s, x)
-                pass_on(z + s, s, False, True)
-
-        if s == 0:
-            arrive(z, 1 - x)
-            multiply(z)
-        else:
-
-            @pl.when(z - s >= 0)
-            def _():
-                arrive(z - s, 1 - x)
-                multiply(z - s)
-
-            @pl.when(z + s < nz)
-            def _():
-                arrive(z + s, 1 - x)
-                multiply(z + s)
+    def pass_on(zz, h):
+        arrive(zz, x, h)
+        across(zz, h)
+
+    def finish(zz):
+        arrive(zz, 1 - x, 0)
+        arrive(zz, 1 - x, 1)
+        multiply(zz)
+
+    for s in range(1, nz):
+        for h in range(2):
+            at_distance(s, lambda t, h=h: pass_on(t, h))
+    finish(z)
+    for s in range(1, nz):
+        at_distance(s, finish)
 
     def part(k):
         return acc.at[pl.ds(pl.multiple_of(k * width, width), width)]
@@ -260,80 +269,81 @@
     grown = jnp.exp(jnp.minimum(aggregated, 0.0))
     slope = cotangent[...] * grown
     local_grad = dot_split(own_rows, slope, ((0,), (0,)))
-    rows = width // n_dev
-    grad[...] = local_grad.reshape(n_dev, rows, width)
-
-    @pl.loop(1, n_dev)
-    def _(k):
-        d = (me + k) % n_dev
+    grad[...] = local_grad
+    n_plane = 2 * n_col
+    rows = width // n_plane
+    mine = x * n_col + j
+
+    def piece(k):
+        return pl.ds(pl.multiple_of(k * rows, rows), rows)
+
+    def member(k):
+        return {"row": z * 2 + k // n_col, "col": k % n_col}
+
+    for k in range(1, n_plane):
+        other = (mine + k) % n_plane
         pltpu.make_async_remote_copy(
-            src_ref=grad.at[d],
-            dst_ref=terms.at[n_dev - 1 - k],
+            src_ref=grad.at[piece(other)],
+            dst_ref=terms.at[n_plane - 1 - k],
             send_sem=term_send,
             recv_sem=term_recv,
-            device_id=device(d),
+            device_id=member(other),
             device_id_type=MESH,
         ).start()
 
     hidden_out[...] = jnp.where(aggregated > 0.0, aggregated, grown - 1.0)
     pltpu.make_async_copy(terms, terms, term_recv).wait()
-    total[...] = grad[me] + jnp.sum(terms[...], axis=0)
-
-    @pl.loop(1, n_dev)
-    def _(k):
-        d = (me + k) % n_dev
+    layers[z] = grad[piece(mine)] + jnp.sum(terms[...], axis=0)
+    for s in range(1, nz):
         pltpu.make_async_remote_copy(
-            src_ref=total,
-            dst_ref=grad_all.at[me],
+            src_ref=layers.at[z],
+            dst_ref=layers.at[z],
+            send_sem=layer_send,
+            recv_sem=layer_recv,
+            device_id={"row": (i + 2 * s) % n_row, "col": j},
+            device_id_type=MESH,
+        ).start()
+    others = layers.at[pl.ds(0, nz - 1)]
+    pltpu.make_async_copy(others, others, layer_recv).wait()
+    weight_grad[piece(mine)] = jnp.sum(layers[...], axis=0)
+    for k in range(1, n_plane):
+        pltpu.make_async_remote_copy(
+            src_ref=weight_grad.at[piece(mine)],
+            dst_ref=weight_grad.at[piece(mine)],
             send_sem=all_send,
             recv_sem=all_recv,
-            device_id=device(d),
+            device_id=member((mine + k) % n_plane),
             device_id_type=MESH,
         ).start()
 
     pltpu.make_async_copy(terms, terms, all_recv).wait()
-    grad_all[me] = total[...]
-    weight_grad[...] = grad_all[...].reshape(width, width)
 
     pltpu.make_async_copy(terms, terms, term_send).wait()
+    pltpu.make_async_copy(others, others, layer_send).wait()
     pltpu.make_async_copy(terms, terms, all_send).wait()
-    send(z, i, across_sem.at[z]).wait_send()
     far_core.wait_send()
     own_core.wait_send()
     y_copy.wait_send()
 
-    def sent(sem):
-        pltpu.make_async_copy(block(0, 0), block(0, 0), sem).wait()
-
-    for s in range(nz):
-        if s > 0:
-
-            @pl.when(z - s >= 0)
-            def _():
-                sent(across_sem.at[z - s])
-
-            @pl.when(z + s < nz)
-            def _():
-                sent(across_sem.at[z + s])
-
-        @pl.when((z - s >= 0) & (z + 1 < nz))
-        def _():
-            sent(up_sem.at[s])
-
-        @pl.when((z + s < nz) & (z > 0))
-        def _():
-            sent(down_sem.at[s])
+    def sent(sem, h):
+        pltpu.make_async_copy(block(0, 0, h), block(0, 0, h), sem).wait()
+
+    for h in range(2):
+        sent(across_sem.at[z, h], h)
+        for s in range(1, nz):
+            at_distance(s, lambda t, h=h: sent(across_sem.at[t, h], h))
+            at_distance(s, lambda t, h=h: sent(line_sem.at[t, h], h))
 
 
 def dense(features, weight, degree, tiles, tile_coords, tile_count, cotangent):
     n_row = lax.axis_size("row")
     n_col = lax.axis_size("col")
-    n_dev = n_row * n_col
     nz = n_row // 2
     width, feat = features.shape
     slots = tiles.shape[2]
-    rows = width // n_dev
+    rows = width // (2 * n_col)
     vmem = pl.BlockSpec(memory_space=pltpu.VMEM)
+    hbm = pl.BlockSpec(memory_space=pltpu.HBM)
     smem = pl.BlockSpec(memory_space=pltpu.SMEM)
     dma = pltpu.SemaphoreType.DMA
     return pl.pallas_call(
@@ -342,9 +352,13 @@
             jax.ShapeDtypeStruct((width, feat), F32),
             jax.ShapeDtypeStruct((feat, feat), F32),
         ),
-        in_specs=[vmem, vmem, vmem, pl.BlockSpec(memory_space=pl.ANY), smem, smem, vmem],
+        in_specs=[hbm, hbm, hbm, hbm, smem, smem, hbm],
         out_specs=(vmem, vmem),
         scratch_shapes=[
+            pltpu.VMEM((width, feat), F32),
+            pltpu.VMEM((feat, feat), F32),
+            pltpu.VMEM((1, width), jnp.int32),
+            pltpu.VMEM((width, feat), F32),
             pltpu.VMEM((slots, width, width), F32),
             pltpu.VMEM((nz, 2 * width, feat), F32),
             pltpu.VMEM((nz, n_col * width, 2 * width), BF16),
@@ -353,16 +367,14 @@
             pltpu.VMEM((2, width, feat), F32),
             pltpu.VMEM((width, feat), F32),
             pltpu.VMEM((width, feat), F32),
-            pltpu.VMEM((n_dev, rows, feat), F32),
-            pltpu.VMEM((n_dev - 1, rows, feat), F32),
-            pltpu.VMEM((rows, feat), F32),
-            pltpu.VMEM((n_dev, rows, feat), F32),
+            pltpu.VMEM((width, feat), F32),
+            pltpu.VMEM((2 * n_col - 1, rows, feat), F32),
+            pltpu.VMEM((nz, rows, feat), F32),
             pltpu.SMEM((slots,), jnp.int32),
-            dma,
-            dma((nz,)),
-            dma((nz,)),
-            dma((nz,)),
+            dma((5,)),
             dma((nz, 2)),
+            dma((nz, 2)),
+            dma((nz, 2, 2)),
             dma((2,)),
             dma((2,)),
             dma,
@@ -371,11 +383,21 @@
             dma,
             dma,
             dma,
+            dma,
+            dma,
         ],
         compiler_params=pltpu.CompilerParams(
-            collective_id=0, has_side_effects=True, vmem_limit_bytes=32 * 1024 * 1024
+            collective_id=0, has_side_effects=True, vmem_limit_bytes=62 * 1024 * 1024
         ),
-    )(features, weight, degree.reshape(1, width), tiles, tile_coords, tile_count, cotangent)
+    )(
+        features,
+        weight,
+        degree.reshape(1, width),
+        tiles,
+        tile_coords[0, 0].T,
+        tile_count,
+        cotangent,
+    )
 
 
 def solution(mesh):
@@ -384,7 +406,7 @@
     def local(features, weight, degree, tiles, tile_coords, tile_count, cotangent):
         width, feat = features.shape
         small = n_row * n_col <= 2 * tiles.shape[2] and n_row % 2 == 0 and n_col == 4
-        small = small and tiles.shape[3] == width and width % (n_row * n_col) == 0
+        small = small and tiles.shape[3] == width and width % (32 * n_col) == 0
         form = dense if small and feat == width else gathered
         return form(features, weight, degree, tiles, tile_coords, tile_count, cotangent)
 

time: 44.8 us -> 36.7 us (0.82)
  Pallas kernels: 36.6 us -> 32.3 us
  local copies, waits for them, and re-layouts: 6.6 us -> 2.95 us
    pallas_call x1, Pallas kernels: 36.6 us -> 32.3 us  [dense(): pl.pallas_call(functools.partial(fused, n_row), out_shape=(jax.ShapeDtype...]
    unnamed x13 -> x2, local copies, waits for them, and re-layouts: 6.6 us -> 2.95 us
where the time goes in v2:
time: 36.7 us; the launch traced here: 36.5 us
  Pallas kernels  32.3 us (88%)
  local copies, waits for them, and re-layouts  2.95 us (8%)
  between operations  1.29 us (4%)
    pallas_call x1, Pallas kernels, dense(): pl.pallas_call(functools.partial(fused, n_row), out_shape=(jax.ShapeDtype...  32.3 us
    unnamed x2, local copies, waits for them, and re-layouts  2.95 us

profile of v2, /device:TPU:0, one launch (start us, length us, event | category | flops | bytes accessed | tf_op | source)
XLA Modules:
  0.0 36.5 jit_solution(10144570794937188925)
XLA Ops:
  1.3 32.3 %shard_map.86 = (f32[128,128]{1,0:T(8,128)}, f32[128,128]{1,0:T(8,128)}) custom-call(f32[128,128]{1,0:T(8,128)} %features_hbm.1, f32[128,128]{1,0:T(8,128)} %weight_hbm.1, s32[1,128]{1,0:T(1,128)} %bitcast.5, f32[1,1,24,128,128]{4,3,2,1,0:T(8,128)} %tiles_hbm.1, s32[2,24]{1,0:T(2,128)} %bitcast.4, s32[1,1]{1,0:T(1,128)S(6)} %copy.11.count, ...), custom_call_target="tpu_custom_call" | custom-call | tf_op jit(solution)/shard_map/pallas_call | solution.py:349
  33.5 1.5 %copy.12 = f32[128,128]{1,0:T(8,128)} copy(f32[128,128]{1,0:T(8,128)} %get-tuple-element.4) | data formatting | bytes 131072
  35.0 1.5 %copy.13 = f32[128,128]{1,0:T(8,128)} copy(f32[128,128]{1,0:T(8,128)} %get-tuple-element.5) | data formatting | bytes 131072

commit v3 on v2

--- a/solution.py
+++ b/solution.py
@@ -348,10 +348,7 @@
     dma = pltpu.SemaphoreType.DMA
     return pl.pallas_call(
         functools.partial(fused, n_row),
-        out_shape=(
-            jax.ShapeDtypeStruct((width, feat), F32),
-            jax.ShapeDtypeStruct((feat, feat), F32),
-        ),
+        out_shape=(pltpu.VMEM((width, feat), F32), pltpu.VMEM((feat, feat), F32)),
         in_specs=[hbm, hbm, hbm, hbm, smem, smem, hbm],
         out_specs=(vmem, vmem),
         scratch_shapes=[
@@ -387,7 +384,7 @@
             dma,
         ],
         compiler_params=pltpu.CompilerParams(
-            collective_id=0, has_side_effects=True, vmem_limit_bytes=62 * 1024 * 1024
+            collective_id=0, has_side_effects=True, vmem_limit_bytes=56 * 1024 * 1024
         ),
     )(
         features,

time: 36.7 us -> 34.3 us (0.935)
  local copies, waits for them, and re-layouts: 2.95 us -> 1.26 us
  Pallas kernels: 32.3 us -> 31.6 us
    unnamed x2, local copies, waits for them, and re-layouts: 2.95 us -> 1.26 us
    pallas_call x1, Pallas kernels: 32.3 us -> 31.6 us  [dense(): pl.pallas_call(functools.partial(fused, n_row), out_shape=(pltpu.VMEM((wi...]
where the time goes in v3:
time: 34.3 us; the launch traced here: 34.2 us
  Pallas kernels  31.6 us (92%)
  between operations  1.29 us (4%)
  local copies, waits for them, and re-layouts  1.26 us (4%)
    pallas_call x1, Pallas kernels, dense(): pl.pallas_call(functools.partial(fused, n_row), out_shape=(pltpu.VMEM((wi...  31.6 us
    unnamed x2, local copies, waits for them, and re-layouts  1.26 us

profile of v3, /device:TPU:0, one launch (start us, length us, event | category | flops | bytes accessed | tf_op | source)
XLA Modules:
  0.0 34.2 jit_solution(8315836119170737301)
XLA Ops:
  1.3 31.6 %shard_map.86 = (f32[128,128]{1,0:T(8,128)S(1)}, f32[128,128]{1,0:T(8,128)S(1)}) custom-call(f32[128,128]{1,0:T(8,128)} %features_hbm.1, f32[128,128]{1,0:T(8,128)} %weight_hbm.1, s32[1,128]{1,0:T(1,128)} %bitcast.5, f32[1,1,24,128,128]{4,3,2,1,0:T(8,128)} %tiles_hbm.1, s32[2,24]{1,0:T(2,128)} %bitcast.4, s32[1,1]{1,0:T(1,128)S(6)} %copy.13.count, ...), custom_call_target="tpu_custom_call" | custom-call | tf_op jit(solution)/shard_map/pallas_call | solution.py:349
  32.9 0.6 %copy.11 = f32[128,128]{1,0:T(8,128)} copy(f32[128,128]{1,0:T(8,128)S(1)} %get-tuple-element.2) | data formatting | bytes 131072
  33.5 0.6 %copy.12 = f32[128,128]{1,0:T(8,128)} copy(f32[128,128]{1,0:T(8,128)S(1)} %get-tuple-element.3) | data formatting | bytes 131072

commit v4 on v3

--- a/solution.py
+++ b/solution.py
@@ -93,8 +93,7 @@
     layers,
     codes,
     load_sem,
-    line_sem,
-    across_sem,
+    send_sem,
     node_sem,
     core_send,
     core_recv,
@@ -183,13 +182,13 @@
             act(z - s)
 
     def across(zz, h):
-        send(zz, h, z * 2 + 1 - x, across_sem.at[zz, h]).start()
+        send(zz, h, z * 2 + 1 - x, send_sem).start()
 
     for h in range(2):
         across(z, h)
     for s in range(nz - 1, 0, -1):
         for h in range(2):
-            at_distance(s, lambda t, h=h: send(z, h, t * 2 + x, line_sem.at[t, h]).start())
+            at_distance(s, lambda t, h=h: send(z, h, t * 2 + x, send_sem).start())
 
     for t in range(slots):
         live = t < count[0, 0]
@@ -325,14 +324,8 @@
     own_core.wait_send()
     y_copy.wait_send()
 
-    def sent(sem, h):
-        pltpu.make_async_copy(block(0, 0, h), block(0, 0, h), sem).wait()
-
-    for h in range(2):
-        sent(across_sem.at[z, h], h)
-        for s in range(1, nz):
-            at_distance(s, lambda t, h=h: sent(across_sem.at[t, h], h))
-            at_distance(s, lambda t, h=h: sent(line_sem.at[t, h], h))
+    sent = tiles.at[pl.ds(0, n_row - 1)]
+    pltpu.make_async_copy(sent, sent, send_sem).wait()
 
 
 def dense(features, weight, degree, tiles, tile_coords, tile_count, cotangent):
@@ -369,8 +362,7 @@
             pltpu.VMEM((nz, rows, feat), F32),
             pltpu.SMEM((slots,), jnp.int32),
             dma((5,)),
-            dma((nz, 2)),
-            dma((nz, 2)),
+            dma,
             dma((nz, 2, 2)),
             dma((2,)),
             dma((2,)),
@@ -403,7 +395,7 @@
     def local(features, weight, degree, tiles, tile_coords, tile_count, cotangent):
         width, feat = features.shape
         small = n_row * n_col <= 2 * tiles.shape[2] and n_row % 2 == 0 and n_col == 4
-        small = small and tiles.shape[3] == width and width % (32 * n_col) == 0
+        small = small and tiles.shape[3] == width and width % (32 * n_col) == 0 and n_row <= tiles.shape[2]
         form = dense if small and feat == width else gathered
         return form(features, weight, degree, tiles, tile_coords, tile_count, cotangent)
 

time: 34.3 us -> 34.1 us (level)
  no operation moved by 1% of the time
where the time goes in v4:
time: 34.1 us; the launch traced here: 34 us
  Pallas kernels  31.4 us (92%)
  between operations  1.29 us (4%)
  local copies, waits for them, and re-layouts  1.26 us (4%)
    pallas_call x1, Pallas kernels, dense(): pl.pallas_call(functools.partial(fused, n_row), out_shape=(pltpu.VMEM((wi...  31.4 us
    unnamed x2, local copies, waits for them, and re-layouts  1.26 us

profile of v4, /device:TPU:0, one launch (start us, length us, event | category | flops | bytes accessed | tf_op | source)
XLA Modules:
  0.0 34.0 jit_solution(11824572552647550943)
XLA Ops:
  1.3 31.4 %shard_map.86 = (f32[128,128]{1,0:T(8,128)S(1)}, f32[128,128]{1,0:T(8,128)S(1)}) custom-call(f32[128,128]{1,0:T(8,128)} %features_hbm.1, f32[128,128]{1,0:T(8,128)} %weight_hbm.1, s32[1,128]{1,0:T(1,128)} %bitcast.5, f32[1,1,24,128,128]{4,3,2,1,0:T(8,128)} %tiles_hbm.1, s32[2,24]{1,0:T(2,128)} %bitcast.4, s32[1,1]{1,0:T(1,128)S(6)} %copy.13.count, ...), custom_call_target="tpu_custom_call" | custom-call | tf_op jit(solution)/shard_map/pallas_call | solution.py:342
  32.7 0.6 %copy.11 = f32[128,128]{1,0:T(8,128)} copy(f32[128,128]{1,0:T(8,128)S(1)} %get-tuple-element.2) | data formatting | bytes 131072
  33.4 0.6 %copy.12 = f32[128,128]{1,0:T(8,128)} copy(f32[128,128]{1,0:T(8,128)S(1)} %get-tuple-element.3) | data formatting | bytes 131072

commit v5 on v4

--- a/solution.py
+++ b/solution.py
@@ -154,7 +154,7 @@
     nodes[z, pl.ds(pl.multiple_of(x * width, width), width)] = features[...] * inv_root
     pl.semaphore_wait(barrier, len(friends))
 
-    step = width // 2
+    step = width // 4
 
     def block(zz, xx, h):
         return nodes.at[zz, pl.ds(pl.multiple_of(xx * width + h * step, step), step)]
@@ -184,10 +184,10 @@
     def across(zz, h):
         send(zz, h, z * 2 + 1 - x, send_sem).start()
 
-    for h in range(2):
+    for h in range(4):
         across(z, h)
     for s in range(nz - 1, 0, -1):
-        for h in range(2):
+        for h in range(4):
             at_distance(s, lambda t, h=h: send(z, h, t * 2 + x, send_sem).start())
 
     for t in range(slots):
@@ -221,12 +221,12 @@
         across(zz, h)
 
     def finish(zz):
-        arrive(zz, 1 - x, 0)
-        arrive(zz, 1 - x, 1)
+        for h in range(4):
+            arrive(zz, 1 - x, h)
         multiply(zz)
 
     for s in range(1, nz):
-        for h in range(2):
+        for h in range(4):
             at_distance(s, lambda t, h=h: pass_on(t, h))
     finish(z)
     for s in range(1, nz):
@@ -363,7 +363,7 @@
             pltpu.SMEM((slots,), jnp.int32),
             dma((5,)),
             dma,
-            dma((nz, 2, 2)),
+            dma((nz, 2, 4)),
             dma((2,)),
             dma((2,)),
             dma,

time: 34.1 us -> 34.2 us (level)
  no operation moved by 1% of the time
where the time goes in v5:
time: 34.2 us; the launch traced here: 34 us
  Pallas kernels  31.5 us (92%)
  between operations  1.29 us (4%)
  local copies, waits for them, and re-layouts  1.26 us (4%)
    pallas_call x1, Pallas kernels, dense(): pl.pallas_call(functools.partial(fused, n_row), out_shape=(pltpu.VMEM((wi...  31.5 us
    unnamed x2, local copies, waits for them, and re-layouts  1.26 us

profile of v5, /device:TPU:0, one launch (start us, length us, event | category | flops | bytes accessed | tf_op | source)
XLA Modules:
  0.0 34.0 jit_solution(3543881222640464923)
XLA Ops:
  1.3 31.5 %shard_map.86 = (f32[128,128]{1,0:T(8,128)S(1)}, f32[128,128]{1,0:T(8,128)S(1)}) custom-call(f32[128,128]{1,0:T(8,128)} %features_hbm.1, f32[128,128]{1,0:T(8,128)} %weight_hbm.1, s32[1,128]{1,0:T(1,128)} %bitcast.5, f32[1,1,24,128,128]{4,3,2,1,0:T(8,128)} %tiles_hbm.1, s32[2,24]{1,0:T(2,128)} %bitcast.4, s32[1,1]{1,0:T(1,128)S(6)} %copy.13.count, ...), custom_call_target="tpu_custom_call" | custom-call | tf_op jit(solution)/shard_map/pallas_call | solution.py:342
  32.8 0.6 %copy.11 = f32[128,128]{1,0:T(8,128)} copy(f32[128,128]{1,0:T(8,128)S(1)} %get-tuple-element.2) | data formatting | bytes 131072
  33.4 0.6 %copy.12 = f32[128,128]{1,0:T(8,128)} copy(f32[128,128]{1,0:T(8,128)S(1)} %get-tuple-element.3) | data formatting | bytes 131072
